TPU v7x, 256 devices: a whole 4x4x8 slice. The times are simulated.
256 devices in a mesh: expert: 8 (over y, x_lo), dp: 32 (over x_hi, z, core).
Axes of the slice: x: 4 (x_hi: 2, x_lo: 2; x = x_hi * 2 + x_lo), y: 4, z: 8, core: 2. Of those that a mesh axis runs over, the one named last changes fastest.
Arguments:
- tokens: bfloat16 [4096, 3072], P(('expert', 'dp')), may hold values from -6 to 6
- cotangent: bfloat16 [4096, 3072], P(('expert', 'dp')), may hold values from -6 to 6
- experts: int32 [4096, 2], P(('expert', 'dp')), may hold values from 0 to 7, all different within a row; in each aligned block of 16 rows (0 to 15, 16 to 31, ...) at most 8 rows name the same one
- gate_weights: float32 [4096, 2], P(('expert', 'dp')), may hold values from 0.1 to 1
- w_up: bfloat16 [8, 3072, 8192], P('expert', None, 'dp'), may hold values from -0.109375 to 0.109375
- master: float32 [8, 8192, 3072], P(None, 'dp', 'expert'), may hold values from -6 to 6
- moment_one: bfloat16 [8, 8192, 3072], P(None, 'dp', 'expert'), may hold values from -18 to 18
- moment_two: bfloat16 [8, 8192, 3072], P(None, 'dp', 'expert'), may hold values from 10 to 100
Outputs:
- new_master: float32 [8, 8192, 3072], P('expert', 'dp')
Inputs may be any that keep to these rules, and one draw needn't show every extreme that they name: Each token names two different experts; the tokens of one device name any expert at most 8 times, a bound that some block reaches.
All inputs are finite; a program needn't handle non-finite values.
Results may differ from a plain program's by a relative error of at most 0.0003.
Values may be sent and summed in bfloat16 or wider, within the bound.
A program may use at most 128 MiB of HBM per device.

v0:
```python
import jax
import jax.numpy as jnp
from jax import lax
from jax.sharding import PartitionSpec as P

CAP = 8
beta_one = 0.9
beta_two = 0.95
corr_one = 1.0 - (0.9**50) ** 2
corr_two = 1.0 - (0.95**50) ** 2
learn_rate = 0.2
weight_decay = 0.1
epsilon = 1e-08


def adam_update(master, moment_one, moment_two, gradient):
    first = beta_one * moment_one.astype(jnp.float32) + (1.0 - beta_one) * gradient
    second = beta_two * moment_two.astype(jnp.float32) + (1.0 - beta_two) * gradient * gradient
    update = first / corr_one / (jnp.sqrt(second / corr_two) + epsilon)
    return master - learn_rate * (update + weight_decay * master)


def body(tokens, cotangent, experts, gate_weights, w_up, master, moment_one, moment_two):
    count_experts = master.shape[0]
    model_width = tokens.shape[1]
    choices_each = experts.shape[1]
    flat_ids = experts.reshape(-1)
    onehot = (flat_ids[:, None] == jnp.arange(count_experts, dtype=jnp.int32)[None, :]).astype(
        jnp.int32
    )
    position = jnp.sum((jnp.cumsum(onehot, axis=0) - 1) * onehot, axis=1)
    target = flat_ids * CAP + position
    placing = (jnp.arange(count_experts * CAP, dtype=jnp.int32)[:, None] == target[None, :]).astype(
        jnp.bfloat16
    )
    token_copies = jnp.repeat(tokens, choices_each, axis=0)
    scaled = (
        jnp.repeat(cotangent.astype(jnp.float32), choices_each, axis=0)
        * gate_weights.reshape(-1)[:, None]
    ).astype(jnp.bfloat16)
    send_tokens = jnp.dot(placing, token_copies, preferred_element_type=jnp.float32).astype(
        jnp.bfloat16
    )
    send_scaled = jnp.dot(placing, scaled, preferred_element_type=jnp.float32).astype(jnp.bfloat16)
    send_tokens = send_tokens.reshape(count_experts, CAP, model_width)
    send_scaled = send_scaled.reshape(count_experts, CAP, model_width)
    got_tokens, got_scaled = (
        lax.all_to_all(send_tokens, "expert", split_axis=0, concat_axis=0, tiled=True),
        lax.all_to_all(send_scaled, "expert", split_axis=0, concat_axis=0, tiled=True),
    )
    got_tokens = got_tokens.reshape(-1, model_width)
    got_scaled = got_scaled.reshape(-1, model_width)
    local_up = w_up[0]
    piece_tokens = lax.all_gather(got_tokens, "dp", axis=0, tiled=True)
    piece_scaled = lax.all_gather(got_scaled, "dp", axis=0, tiled=True)
    hidden = jax.nn.silu(
        jnp.dot(piece_tokens, local_up, preferred_element_type=jnp.float32)
    ).astype(jnp.bfloat16)
    gradient = lax.dot_general(
        hidden, piece_scaled, (((0,), (0,)), ((), ())), preferred_element_type=jnp.float32
    )
    gradient = gradient[None]
    spread = lax.all_to_all(
        gradient.astype(jnp.bfloat16), "expert", split_axis=2, concat_axis=0, tiled=True
    ).astype(gradient.dtype)
    fresh_master = adam_update(master, moment_one, moment_two, spread)
    return lax.all_to_all(fresh_master, "expert", split_axis=0, concat_axis=2, tiled=True)


def solution(mesh):
    placed = (
        P(("expert", "dp"), None),
        P(("expert", "dp"), None),
        P(("expert", "dp"), None),
        P(("expert", "dp"), None),
        P("expert", None, "dp"),
        P(None, "dp", "expert"),
        P(None, "dp", "expert"),
        P(None, "dp", "expert"),
    )
    return jax.shard_map(
        body, mesh=mesh, in_specs=placed, out_specs=P("expert", "dp", None), check_vma=False
    )
```

profile of v0, /device:TPU:1, one launch (start us, length us, event | category | flops | bytes accessed | tf_op | source)
XLA Modules:
  0.0 399.0 jit_solution(3929386972154533601)
XLA Ops:
  6.5 0.9 copy.17
  7.4 0.1 reshape.36
  7.7 0.2 select_reduce_fusion
  7.8 1.0 broadcast_in_dim.5
  8.9 0.3 reshape.40
  9.1 0.8 copy.18
  10.0 0.3 fusion.2
  10.3 13.6 %all_to_all.37 = bf16[8,8,3072]{2,1,0:T(8,128)(2,1)} all-to-all(bf16[8,8,3072]{2,1,0:T(8,128)(2,1)S(1)} %fusion.2), channel_id=1, replica_groups=mesh['expert'=8,'dp'=32] {'expert'}, dimensions={0} | all-to-all | bytes 786432 | tf_op jit(solution)/shard_map/all_to_all | solution.py:49
  24.0 0.1 broadcast_in_dim.4
  24.2 0.2 fusion.1
  24.4 10.1 %all_to_all.38 = bf16[8,8,3072]{2,1,0:T(8,128)(2,1)} all-to-all(bf16[8,8,3072]{2,1,0:T(8,128)(2,1)S(1)} %fusion.1), channel_id=1, replica_groups=mesh['expert'=8,'dp'=32] {'expert'}, dimensions={0} | all-to-all | bytes 786432 | tf_op jit(solution)/shard_map/all_to_all | solution.py:48
  34.6 109.2 %all-gather.5.cloned.1.call-done = bf16[2048,3072]{1,0:T(8,128)(2,1)} async-done(((bf16[64,3072]{1,0:T(8,128)(2,1)}), bf16[2048,3072]{1,0:T(8,128)(2,1)}) %all-gather.5.cloned.1.call-update) | async-done | bytes 12582928 | tf_op jit(solution)/shard_map/all_gather | solution.py:55
  143.8 117.0 %all-gather.3.cloned.1.call-done = bf16[2048,3072]{1,0:T(8,128)(2,1)} async-done(((bf16[64,3072]{1,0:T(8,128)(2,1)}), bf16[2048,3072]{1,0:T(8,128)(2,1)}) %all-gather.3.cloned.1.call-update) | async-done | bytes 12582928 | tf_op jit(solution)/shard_map/all_gather | solution.py:54
  260.8 21.1 %fusion = bf16[1,256,3072]{2,1,0:T(8,128)(2,1)S(1)} fusion(bf16[2048,3072]{1,0:T(8,128)(2,1)} %all-gather.5.cloned.1.call-done, bf16[2048,3072]{1,0:T(8,128)(2,1)} %all-gather.3.cloned.1.call-done, bf16[1,3072,256]{2,1,0:T(8,128)(2,1)S(1)} %copy-done), kind=kOutput, calls=%fused_computation.2 | convolution fusion | flops 6445858816 | bytes 28311552 | tf_op jit(solution)/shard_map/dot_general | solution.py:59
  281.9 5.2 %copy.19 = bf16[1,256,3072]{1,0,2:T(2,128)(2,1)} copy(bf16[1,256,3072]{2,1,0:T(8,128)(2,1)S(1)} %fusion) | data formatting | bytes 3145728 | tf_op jit(solution)/shard_map/convert_element_type | solution.py:64
  287.1 0.5 broadcast.23
  287.6 16.7 %reduce = bf16[3072,256]{1,0:T(8,128)(2,1)S(1)} reduce(bf16[3072,1,256]{2,1,0:T(2,128)(2,1)} %bitcast.40, bf16[]{:T(256)} %broadcast.23), dimensions={1}, to_apply=%bitcast.35.reduce_sub_computation | reduce | bytes 3145730
  304.3 1.8 reshape.45
  306.1 24.6 %all_to_all.39 = bf16[8,2,49152]{2,1,0:T(2,128)(2,1)S(1)} all-to-all(bf16[8,2,49152]{2,1,0:T(2,128)(2,1)} %reshape.45), channel_id=1, replica_groups=mesh['expert'=8,'dp'=32] {'expert'}, dimensions={0} | all-to-all | bytes 3145728 | tf_op jit(solution)/shard_map/all_to_all | solution.py:63
  330.7 3.9 reshape.46
  334.6 8.8 %copy.20 = f32[1,256,8,384]{3,1,2,0:T(8,128)} copy(bf16[1,256,8,384]{1,0,3,2:T(2,128)(2,1)} %bitcast.41) | data formatting | bytes 4718592 | tf_op jit(solution)/shard_map/convert_element_type | solution.py:65
  343.4 5.8 %multiply_subtract_fusion = f32[8,256,384]{2,1,0:T(8,128)S(1)} fusion(f32[8,256,384]{2,1,0:T(8,128)} %param.13, f32[1,256,8,384]{3,1,2,0:T(8,128)} %copy.20, bf16[8,256,384]{2,1,0:T(8,128)(2,1)S(1)} %copy-done.1, bf16[8,256,384]{2,1,0:T(8,128)(2,1)} %param.14), kind=kLoop, calls=%fused_computation.16 | loop fusion | flops 13369344 | bytes 12582912 | tf_op jit(solution)/shard_map/sub | solution.py:20
  349.2 40.9 %all_to_all.40 = f32[8,256,384]{2,1,0:T(8,128)S(1)} all-to-all(f32[8,256,384]{2,1,0:T(8,128)S(1)} %multiply_subtract_fusion), channel_id=1, replica_groups=mesh['expert'=8,'dp'=32] {'expert'}, dimensions={0} | all-to-all | bytes 6291456 | tf_op jit(solution)/shard_map/all_to_all | solution.py:67
  390.1 2.1 copy.22
  (15 shorter events, 0.4 us)
Async XLA Ops:
  6.5 254.3 %copy-start = (bf16[1,3072,256]{2,1,0:T(8,128)(2,1)S(1)}, bf16[1,3072,256]{2,1,0:T(8,128)(2,1)}, u32[]{:S(2)}) copy-start(bf16[1,3072,256]{2,1,0:T(8,128)(2,1)} %param.12) | copy-start | bytes 4718596
  6.5 17.5 %copy-start.2 = (bf16[16,3072]{1,0:T(8,128)(2,1)S(1)}, bf16[16,3072]{1,0:T(8,128)(2,1)}, u32[]{:S(2)}) copy-start(bf16[16,3072]{1,0:T(8,128)(2,1)} %param.8) | copy-start | bytes 294916
  6.5 137.2 %all-gather.5.cloned.1.call-start = ((), (), s32[]{:S(2)}) async-start(), calls=%async_computation.5 | async-start | bytes 12976128 | tf_op jit(solution)/shard_map/all_gather | solution.py:55
  23.9 236.9 %all-gather.3.cloned.1.call-start = ((), (), s32[]{:S(2)}) async-start(), calls=%async_computation.4 | async-start | bytes 12976128 | tf_op jit(solution)/shard_map/all_gather | solution.py:54
  334.6 8.8 %copy-start.1 = (bf16[8,256,384]{2,1,0:T(8,128)(2,1)S(1)}, bf16[8,256,384]{2,1,0:T(8,128)(2,1)}, u32[]{:S(2)}) copy-start(bf16[8,256,384]{2,1,0:T(8,128)(2,1)} %param.15) | copy-start | bytes 4718596
Sparse Core Ops, SparseCore 0:
  24.1 119.6 all-gather.4
  146.5 114.2 all-gather.2
where the time goes:
time: 400 us; the launch traced here: 399 us
  waiting for transfers between devices  226 us (56%)
  blocking collectives  89.2 us (22%)
  local copies, waits for them, and re-layouts  25.5 us (6%)
  other arithmetic  22.8 us (6%)
  matrix products  21.7 us (5%)
  between operations  13.5 us (3%)
    all_gather x1, waiting for transfers between devices, body(): piece_tokens = lax.all_gather(got_tokens, 'dp', axis=0, tiled=True)  117 us
    all_gather x1, waiting for transfers between devices, body(): piece_scaled = lax.all_gather(got_scaled, 'dp', axis=0, tiled=True)  109 us
    all_to_all x1, blocking collectives, body(): lax.all_to_all(fresh_master, 'expert', split_axis=0, concat_axis=2, tiled...  40.9 us
    all_to_all x1, blocking collectives, body(): lax.all_to_all(gradient.astype(jnp.bfloat16), 'expert', split_axis=2, con...  24.6 us
    dot_general x1, matrix products, body(): lax.dot_general(hidden, piece_scaled, (((0,), (0,)), ((), ())), preferred...  21.1 us
    unnamed x1, other arithmetic  16.7 us
    all_to_all x1, blocking collectives, body(): lax.all_to_all(send_scaled, 'expert', split_axis=0, concat_axis=0, tiled=...  13.6 us
    all_to_all x1, blocking collectives, body(): lax.all_to_all(send_tokens, 'expert', split_axis=0, concat_axis=0, tiled=...  10.1 us
  transfers between devices with their start and end apart: 2, of which 2 were waited for; matrix products, arithmetic and copies ran while one was open for 0% of the time, Pallas kernels for 0%

commit v1 on v0

--- a/solution.py
+++ b/solution.py
@@ -60,8 +60,14 @@
         hidden, piece_scaled, (((0,), (0,)), ((), ())), preferred_element_type=jnp.float32
     )
     gradient = gradient[None]
-    spread = lax.all_to_all(
-        gradient.astype(jnp.bfloat16), "expert", split_axis=2, concat_axis=0, tiled=True
+    spread = jnp.concatenate(
+        lax.all_to_all(
+            jnp.stack(jnp.split(gradient.astype(jnp.bfloat16), lax.axis_size("expert"), axis=2)),
+            "expert",
+            0,
+            0,
+        ),
+        axis=0,
     ).astype(gradient.dtype)
     fresh_master = adam_update(master, moment_one, moment_two, spread)
     return lax.all_to_all(fresh_master, "expert", split_axis=0, concat_axis=2, tiled=True)

time: 400 us -> 364 us (0.910)
  other arithmetic: 22.8 us -> 4.37 us
  local copies, waits for them, and re-layouts: 25.5 us -> 9.94 us
    unnamed x1 -> x0, other arithmetic: 16.7 us -> none
    convert_element_type x2 -> x0, local copies, waits for them, and re-layouts: 14 us -> none  [the longest x1 8.81 us: body(): spread = lax.all_to_all(gradient.astype(jnp.bfloat16), 'expert', split_ax...]
    all_gather x1, waiting for transfers between devices: 117 us -> 109 us  [body(): piece_tokens = lax.all_gather(got_tokens, 'dp', axis=0, tiled=True)]
    all_gather x1, waiting for transfers between devices: 109 us -> 117 us  [body(): piece_scaled = lax.all_gather(got_scaled, 'dp', axis=0, tiled=True)]
    unnamed x11 -> x19, local copies, waits for them, and re-layouts: 7.86 us -> 1.19 us
    all_to_all x1 -> x2, local copies, waits for them, and re-layouts: 2.06 us -> 7.09 us  [body(): lax.all_to_all(fresh_master, 'expert', split_axis=0, concat_axis=2, tiled...]
where the time goes in v1:
time: 364 us
  waiting for transfers between devices  226 us (62%)
  blocking collectives  88.3 us (24%)
  matrix products  21.7 us (6%)
  between operations  13.6 us (4%)
  local copies, waits for them, and re-layouts  9.94 us (3%)
  other arithmetic  4.37 us (1%)
    all_gather x1, waiting for transfers between devices, body(): piece_scaled = lax.all_gather(got_scaled, 'dp', axis=0, tiled=True)  117 us
    all_gather x1, waiting for transfers between devices, body(): piece_tokens = lax.all_gather(got_tokens, 'dp', axis=0, tiled=True)  109 us
    all_to_all x1, blocking collectives, body(): lax.all_to_all(fresh_master, 'expert', split_axis=0, concat_axis=2, tiled...  39.9 us
    all_to_all x1, blocking collectives, body(): lax.all_to_all(jnp.stack(jnp.split(gradient.astype(jnp.bfloat16), lax.axi...  24.7 us
    dot_general x1, matrix products, body(): lax.dot_general(hidden, piece_scaled, (((0,), (0,)), ((), ())), preferred...  21.1 us
    all_to_all x1, blocking collectives, body(): lax.all_to_all(send_tokens, 'expert', split_axis=0, concat_axis=0, tiled=...  13.6 us
    all_to_all x1, blocking collectives, body(): lax.all_to_all(send_scaled, 'expert', split_axis=0, concat_axis=0, tiled=...  10.1 us
  transfers between devices with their start and end apart: 2, of which 2 were waited for; matrix products, arithmetic and copies ran while one was open for 0% of the time, Pallas kernels for 0%

profile of v1, /device:TPU:1, one launch (start us, length us, event | category | flops | bytes accessed | tf_op | source)
XLA Modules:
  0.0 363.7 jit_solution(12717505095565510971)
XLA Ops:
  6.5 0.9 copy.11
  7.4 0.1 reshape.35
  7.5 0.1 fusion.31
  7.6 0.1 reduce_window_sum.11
  7.6 0.2 select_reduce_fusion
  7.8 1.0 broadcast_in_dim.4
  8.8 0.1 reshape.36
  8.9 0.2 fusion.1
  9.2 13.6 %all_to_all.33 = bf16[8,8,3072]{2,1,0:T(8,128)(2,1)} all-to-all(bf16[8,8,3072]{2,1,0:T(8,128)(2,1)S(1)} %fusion.1), channel_id=1, replica_groups=mesh['expert'=8,'dp'=32] {'expert'}, dimensions={0} | all-to-all | bytes 786432 | tf_op jit(solution)/shard_map/all_to_all | solution.py:48
  22.8 0.0 all-gather.5.cloned.1.call-start
  22.9 0.1 copy.12
  22.9 0.1 mul.66
  23.0 0.1 broadcast_in_dim.5
  23.2 0.3 reshape.39
  23.4 0.3 fusion.2
  23.8 10.1 %all_to_all.34 = bf16[8,8,3072]{2,1,0:T(8,128)(2,1)} all-to-all(bf16[8,8,3072]{2,1,0:T(8,128)(2,1)S(1)} %fusion.2), channel_id=1, replica_groups=mesh['expert'=8,'dp'=32] {'expert'}, dimensions={0} | all-to-all | bytes 786432 | tf_op jit(solution)/shard_map/all_to_all | solution.py:49
  33.9 108.7 %all-gather.3.cloned.1.call-done = bf16[2048,3072]{1,0:T(8,128)(2,1)} async-done(((bf16[64,3072]{1,0:T(8,128)(2,1)}), bf16[2048,3072]{1,0:T(8,128)(2,1)}) %all-gather.3.cloned.1.call-update) | async-done | bytes 12582928 | tf_op jit(solution)/shard_map/all_gather | solution.py:54
  142.6 117.0 %all-gather.5.cloned.1.call-done = bf16[2048,3072]{1,0:T(8,128)(2,1)} async-done(((bf16[64,3072]{1,0:T(8,128)(2,1)}), bf16[2048,3072]{1,0:T(8,128)(2,1)}) %all-gather.5.cloned.1.call-update) | async-done | bytes 12582928 | tf_op jit(solution)/shard_map/all_gather | solution.py:55
  259.7 21.1 %fusion = bf16[1,256,3072]{2,1,0:T(8,128)(2,1)S(1)} fusion(bf16[2048,3072]{1,0:T(8,128)(2,1)} %all-gather.5.cloned.1.call-done, bf16[2048,3072]{1,0:T(8,128)(2,1)} %all-gather.3.cloned.1.call-done, bf16[1,3072,256]{2,1,0:T(8,128)(2,1)S(1)} %copy-done), kind=kOutput, calls=%fused_computation.4 | convolution fusion | flops 6445858816 | bytes 28311552 | tf_op jit(solution)/shard_map/dot_general | solution.py:59
  281.1 24.7 %all_to_all.35 = bf16[8,1,256,384]{3,2,1,0:T(8,128)(2,1)S(1)} all-to-all(bf16[8,1,256,384]{3,2,1,0:T(8,128)(2,1)S(1)} %fusion.20), channel_id=1, replica_groups=mesh['expert'=8,'dp'=32] {'expert'}, dimensions={0} | all-to-all | bytes 3145728 | tf_op jit(solution)/shard_map/all_to_all | solution.py:64
  305.8 4.1 %fusion.8 = f32[8,256,384]{2,1,0:T(8,128)S(1)} fusion(f32[8,256,384]{2,1,0:T(8,128)S(1)} %copy-done.1, bf16[8,256,384]{2,1,0:T(8,128)(2,1)S(1)} %copy-done.2, bf16[8,256,384]{2,1,0:T(8,128)(2,1)} %param.14, bf16[8,1,256,384]{3,2,1,0:T(8,128)(2,1)S(1)} %all_to_all.35), kind=kLoop, calls=%fused_computation.14 | loop fusion | flops 14155776 | bytes 11010048 | tf_op jit(solution)/shard_map/sub | solution.py:20
  309.8 39.9 %all_to_all.36 = f32[8,256,384]{2,1,0:T(8,128)} all-to-all(f32[8,256,384]{2,1,0:T(8,128)S(1)} %fusion.8), channel_id=1, replica_groups=mesh['expert'=8,'dp'=32] {'expert'}, dimensions={0} | all-to-all | bytes 6291456 | tf_op jit(solution)/shard_map/all_to_all | solution.py:73
  349.7 3.6 copy.13
  353.3 3.5 copy.14
  (22 shorter events, 0.3 us)
Async XLA Ops:
  6.5 253.1 %copy-start = (bf16[1,3072,256]{2,1,0:T(8,128)(2,1)S(1)}, bf16[1,3072,256]{2,1,0:T(8,128)(2,1)}, u32[]{:S(2)}) copy-start(bf16[1,3072,256]{2,1,0:T(8,128)(2,1)} %param.12) | copy-start | bytes 4718596
  6.5 16.3 %copy-start.4 = (f32[16,2]{0,1:T(2,128)S(1)}, f32[16,2]{0,1:T(2,128)}, u32[]{:S(2)}) copy-start(f32[16,2]{0,1:T(2,128)} %param.11) | copy-start | bytes 388
  6.5 16.5 %copy-start.3 = (bf16[16,3072]{1,0:T(8,128)(2,1)S(1)}, bf16[16,3072]{1,0:T(8,128)(2,1)}, u32[]{:S(2)}) copy-start(bf16[16,3072]{1,0:T(8,128)(2,1)} %param.9) | copy-start | bytes 294916
  6.5 136.1 %all-gather.3.cloned.1.call-start = ((), (), s32[]{:S(2)}) async-start(), calls=%async_computation.4 | async-start | bytes 12976128 | tf_op jit(solution)/shard_map/all_gather | solution.py:54
  22.8 236.9 %all-gather.5.cloned.1.call-start = ((), (), s32[]{:S(2)}) async-start(), calls=%async_computation.5 | async-start | bytes 12976128 | tf_op jit(solution)/shard_map/all_gather | solution.py:55
  280.9 24.9 %copy-start.2 = (bf16[8,256,384]{2,1,0:T(8,128)(2,1)S(1)}, bf16[8,256,384]{2,1,0:T(8,128)(2,1)}, u32[]{:S(2)}) copy-start(bf16[8,256,384]{2,1,0:T(8,128)(2,1)} %param.15) | copy-start | bytes 4718596
  281.0 24.8 %copy-start.1 = (f32[8,256,384]{2,1,0:T(8,128)S(1)}, f32[8,256,384]{2,1,0:T(8,128)}, u32[]{:S(2)}) copy-start(f32[8,256,384]{2,1,0:T(8,128)} %param.13) | copy-start | bytes 9437188
Sparse Core Ops, SparseCore 0:
  22.9 119.6 all-gather.2
  145.4 114.2 all-gather.4
